TPU v7x, 32 devices: a whole 2x2x4 slice. The times are simulated.
32 devices in a mesh: sec: 2 (over core), lat: 4 (over z), lon: 4 (over y, x).
Axes of the slice: x: 2, y: 2, z: 4, core: 2. Of those that a mesh axis runs over, the one named last changes fastest.
Arguments:
- adjoint_end: float32 [3, 16, 256, 1024], P(None, None, 'lat', ('sec', 'lon')), may hold values from -6 to 6
- east_flow: bfloat16 [16, 256, 1024], P(None, 'lat', ('sec', 'lon')), may hold values from -0.079589844 to 0.079589844
- east_diff: bfloat16 [16, 256, 1024], P(None, 'lat', ('sec', 'lon')), may hold values from 0.039794922 to 0.119628906
- north_flow: bfloat16 [16, 256, 1024], P(None, 'lat', ('sec', 'lon')), may hold values from -0.079589844 to 0.079589844
- north_diff: bfloat16 [16, 256, 1024], P(None, 'lat', ('sec', 'lon')), may hold values from 0.039794922 to 0.119628906
- vert_diff: bfloat16 [15, 256, 1024], P(None, 'lat', ('sec', 'lon')), may hold values from 0.019897461 to 0.1796875
- ocean_mask: int32 [256, 1024], P('lat', ('sec', 'lon')), may hold values 0 or 1
- reaction: float32 [3, 3], replicated, may hold values from -0.05 to 0.05
- solubility: float32 [3, 256, 1024], P(None, 'lat', ('sec', 'lon')), may hold values from 0.1 to 1
- route_tile: int32 [8, 256, 1], P(None, 'lat'), may hold values from 0 to 7; in each aligned block of 64 rows (0 to 63, 64 to 127, ..., all dimensions but the last counted through in order) at most 16 rows name the same one
- route_block: int32 [8, 256], P(None, 'lat'), may hold values from 0 to 31
- xgrid_weights: bfloat16 [256, 1024, 128], P('lat', ('sec', 'lon')), may hold values from -0.5 to 0.5
- deposition: bfloat16 [32, 128, 1024], P(None, 'lat', ('sec', 'lon')), may hold values from 0.19921875 to 2
Outputs:
- adjoint_start: float32 [3, 16, 256, 1024], P(None, None, 'lat', ('sec', 'lon'))
- flux_adjoint: float32 [128, 1024], P('lat', ('sec', 'lon'))
- ash_adjoint: float32 [32, 128, 1024], P(None, 'lat', ('sec', 'lon'))
Inputs may be any that keep to these rules, and one draw needn't show every extreme that they name: `route_tile`: among the 64 rows of one device (aligned blocks of 64 rows, in the order of the first two dimensions) no tile is named more than 16 times, a bound that some block reaches.
All inputs are finite; a program needn't handle non-finite values. No bound on the sum of `ocean_mask` on one device may be relied on, other than what follows from the above.
Results may differ from a plain program's by a relative error of at most 0.0029.
Values may be sent and summed in bfloat16 or wider, within the bound.
A program may use at most 128 MiB of HBM per device.

v0:
```python
import jax
import jax.numpy as jnp
from jax import lax
from jax.sharding import PartitionSpec as P

NSTEP = 16


def padded(cells, sides, width, closed):
    for axis, dim in sides:
        count = lax.axis_size(axis)
        ends = count if closed else count - 1
        head = lax.slice_in_dim(cells, 0, width, axis=dim)
        tail = lax.slice_in_dim(cells, cells.shape[dim] - width, cells.shape[dim], axis=dim)
        cells = jnp.concatenate(
            [
                lax.ppermute(tail, axis, [(i, (i + 1) % count) for i in range(ends)]),
                cells,
                lax.ppermute(head, axis, [((i + 1) % count, i) for i in range(ends)]),
            ],
            axis=dim,
        )
    return cells


def edge_masks(row_count, col_count):
    row_ids = jnp.arange(row_count, dtype=jnp.int32)[:, None]
    col_ids = jnp.arange(col_count, dtype=jnp.int32)[None, :]
    return (row_ids == 0, row_ids == row_count - 1, col_ids == 0, col_ids == col_count - 1)


def face_terms(planes, levels):
    row_count = planes.shape[1]
    col_count = planes.shape[2]
    first_row, last_row, first_col, last_col = edge_masks(row_count, col_count)
    row_strip = jnp.stack([planes[:, 0, :], planes[:, -1, :]], 0)
    row_edges = padded(row_strip, (("lat", 0),), 1, False).astype(jnp.float32)
    col_strip = jnp.stack([planes[:, :, 0], planes[:, :, -1]], 0)
    col_edges = padded(col_strip, ((("sec", "lon"), 0),), 1, True).astype(jnp.float32)
    below = row_edges[0]
    above = row_edges[3]
    left = col_edges[0]
    right = col_edges[3]
    full = planes.astype(jnp.float32)
    east_flow = full[0:levels]
    east_diff = full[levels : 2 * levels]
    north_flow = full[2 * levels : 3 * levels]
    north_diff = full[3 * levels : 4 * levels]
    ocean_plane = full[4 * levels]
    ocean_east = jnp.where(last_col, right[4 * levels][:, None], jnp.roll(ocean_plane, -1, axis=1))
    east_open = ocean_plane * ocean_east
    east_fwd = (0.5 * east_flow + east_diff) * east_open
    east_back = (0.5 * east_flow - east_diff) * east_open
    left_open = left[4 * levels] * ocean_plane[:, 0]
    left_back = (0.5 * left[0:levels] - left[levels : 2 * levels]) * left_open
    west_back = jnp.where(first_col, left_back[:, :, None], jnp.roll(east_back, 1, axis=2))
    ocean_north = jnp.where(last_row, above[4 * levels][None, :], jnp.roll(ocean_plane, -1, axis=0))
    north_open = ocean_plane * ocean_north
    north_fwd = (0.5 * north_flow + north_diff) * north_open
    north_back = (0.5 * north_flow - north_diff) * north_open
    below_open = below[4 * levels] * ocean_plane[0]
    below_back = (
        0.5 * below[2 * levels : 3 * levels] - below[3 * levels : 4 * levels]
    ) * below_open
    south_back = jnp.where(first_row, below_back[:, None, :], jnp.roll(north_back, 1, axis=1))
    return (east_fwd, west_back, north_fwd, south_back, ocean_plane)


def advance(adjoint, face_set, vertical, reaction):
    east_fwd, west_back, north_fwd, south_back, ocean_plane = face_set
    tracers, levels, row_count, col_count = adjoint.shape
    first_row, last_row, first_col, last_col = edge_masks(row_count, col_count)
    row_strip = jnp.stack([adjoint[:, :, 0, :], adjoint[:, :, -1, :]], 0)
    row_edges = padded(row_strip, (("lat", 0),), 1, False)
    col_strip = jnp.stack([adjoint[:, :, :, 0], adjoint[:, :, :, -1]], 0).reshape(
        2, tracers * levels * row_count
    )
    col_edges = padded(col_strip, ((("sec", "lon"), 0),), 1, True)
    left = col_edges[0].reshape(tracers, levels, row_count)
    right = col_edges[3].reshape(tracers, levels, row_count)
    east_side = jnp.where(last_col, right[..., None], jnp.roll(adjoint, -1, axis=3))
    west_side = jnp.where(first_col, left[..., None], jnp.roll(adjoint, 1, axis=3))
    upper = jnp.where(last_row, row_edges[3][:, :, None, :], jnp.roll(adjoint, -1, axis=2))
    lower = jnp.where(first_row, row_edges[0][:, :, None, :], jnp.roll(adjoint, 1, axis=2))
    change = (
        east_fwd * (east_side - adjoint)
        + west_back * (adjoint - west_side)
        + north_fwd * (upper - adjoint)
        + south_back * (adjoint - lower)
    )
    vert_flux = vertical * (adjoint[:, 1:] - adjoint[:, :-1])
    boundary = jnp.zeros_like(adjoint[:, :1])
    vert_change = jnp.concatenate([vert_flux, boundary], 1) - jnp.concatenate(
        [boundary, vert_flux], 1
    )
    coupled = jnp.stack(
        [
            sum((reaction[source, tracer] * adjoint[source] for source in range(tracers)))
            for tracer in range(tracers)
        ]
    )
    return ocean_plane * (adjoint + change + vert_change + coupled)


def ocean_blocks(surface_sum, ocean_local, solubility, xgrid_weights):
    tracers = surface_sum.shape[0]
    tracer_sum = sum((solubility[tracer] * surface_sum[tracer] for tracer in range(tracers)))
    flux_ocean = (ocean_local * (tracer_sum * (1.0 / NSTEP))).astype(jnp.bfloat16)
    return jnp.einsum("bo,boa->ba", flux_ocean, xgrid_weights, preferred_element_type=jnp.float32)


def deliver(blocks, route_tile, route_block, atm_rows):
    senders = lax.axis_size(("sec", "lon"))
    own_index = lax.axis_index(("sec", "lon"))
    block_count = blocks.shape[0]
    cell_count = blocks.shape[1]
    capacity = max(2, 2 * block_count // senders)
    dest_tiles = route_tile[:, :, 0]
    peer_ids = jnp.arange(senders, dtype=jnp.int32)
    slot_ids = jnp.arange(capacity, dtype=jnp.int32).astype(jnp.float32)
    own_tiles = lax.dynamic_index_in_dim(dest_tiles, own_index, 0, keepdims=False)
    dest_hot = (own_tiles[:, None] == peer_ids[None, :]).astype(jnp.float32)
    order_rank = jnp.cumsum(dest_hot, axis=0) - dest_hot
    slot_index = jnp.sum(order_rank * dest_hot, axis=1)
    slot_hot = (slot_index[:, None] == slot_ids[None, :]).astype(jnp.float32)
    selector = (dest_hot[:, :, None] * slot_hot[:, None, :]).reshape(
        block_count, senders * capacity
    )
    outgoing = jnp.dot(selector.T, blocks, precision=lax.Precision.HIGHEST).reshape(
        senders, capacity, cell_count
    )
    incoming = lax.all_to_all(outgoing, ("sec", "lon"), split_axis=0, concat_axis=0, tiled=True)
    arrived = (dest_tiles == own_index).astype(jnp.float32)
    arrival_rank = jnp.cumsum(arrived, axis=1) - arrived
    slot_take = arrived[:, :, None] * (arrival_rank[:, :, None] == slot_ids[None, None, :]).astype(
        jnp.float32
    )
    block_hot = (
        route_block[:, :, None] == jnp.arange(atm_rows, dtype=jnp.int32)[None, None, :]
    ).astype(jnp.float32)
    placing = jnp.einsum("syc,sya->asc", slot_take, block_hot, precision=lax.Precision.HIGHEST)
    placing = placing.reshape(atm_rows, senders * capacity)
    return jnp.dot(
        placing, incoming.reshape(senders * capacity, cell_count), precision=lax.Precision.HIGHEST
    )


def per_device(
    adjoint_end,
    east_flow,
    east_diff,
    north_flow,
    north_diff,
    vert_diff,
    ocean_mask,
    reaction,
    solubility,
    route_tile,
    route_block,
    xgrid_weights,
    deposition,
):
    levels = adjoint_end.shape[1]
    atm_rows = deposition.shape[1]
    ocean_local = ocean_mask.astype(jnp.float32)
    mask_plane = ocean_mask.astype(jnp.bfloat16)[None]
    start_sum = jnp.zeros_like(adjoint_end[:, 0])
    planes = jnp.concatenate([east_flow, east_diff, north_flow, north_diff, mask_plane], 0)
    face_set = face_terms(planes, levels)
    vertical = vert_diff.astype(jnp.float32)

    def loop_step(counter, carry):
        adjoint, surface_sum = carry
        surface_sum = surface_sum + adjoint[:, 0]
        return (advance(adjoint, face_set, vertical, reaction), surface_sum)

    adjoint, surface_sum = lax.fori_loop(0, NSTEP - 1, loop_step, (adjoint_end, start_sum))
    surface_sum = surface_sum + adjoint[:, 0]
    blocks = ocean_blocks(surface_sum, ocean_local, solubility, xgrid_weights)
    flux_adjoint = deliver(blocks, route_tile, route_block, atm_rows)
    adjoint_start = advance(adjoint, face_set, vertical, reaction)
    ash_adjoint = deposition.astype(jnp.float32) * flux_adjoint[None]
    return (adjoint_start, flux_adjoint, ash_adjoint)


def solution(mesh):
    in_specs = (
        P(None, None, "lat", ("sec", "lon")),
        P(None, "lat", ("sec", "lon")),
        P(None, "lat", ("sec", "lon")),
        P(None, "lat", ("sec", "lon")),
        P(None, "lat", ("sec", "lon")),
        P(None, "lat", ("sec", "lon")),
        P("lat", ("sec", "lon")),
        P(),
        P(None, "lat", ("sec", "lon")),
        P(None, "lat", None),
        P(None, "lat"),
        P("lat", ("sec", "lon"), None),
        P(None, "lat", ("sec", "lon")),
    )
    out_specs = (
        P(None, None, "lat", ("sec", "lon")),
        P("lat", ("sec", "lon")),
        P(None, "lat", ("sec", "lon")),
    )
    return jax.shard_map(
        per_device, mesh=mesh, in_specs=in_specs, out_specs=out_specs, check_vma=False
    )
```

profile of v0, /device:TPU:0, one launch (start us, length us, event | category | flops | bytes accessed | tf_op | source)
XLA Modules:
  0.0 904.6 jit_solution(17966329856406915420)
XLA Ops:
  52.2 804.8 %while.13 = (s32[]{:T(128)}, f32[3,16,64,128]{3,1,0,2:T(8,128)}, f32[3,64,128]{2,0,1:T(4,128)S(1)}, f32[1,64,128]{2,1,0:T(8,128)}, f32[16,64,128]{2,0,1:T(8,128)...) while((s32[]{:T(128)}, f32[3,16,64,128]{3,1,0,2:T(8,128)}, ...), condition=%wide.region_1.2_spmd.clone, body=%wide.region_0.1_spmd.clone.sunk | while | flops 12976515 | bytes 45655228 | solution.py:177
  82.4 8.1 multiply_add_fusion.7
  94.7 9.5 %fusion.94 = f32[3,16,64,128]{3,1,0,2:T(8,128)} fusion(f32[3,16,64,128]{3,1,0,2:T(8,128)} %get-tuple-element.374, f32[3,16,64,1]{3,1,0,2:T(8,128)} %get-tuple-element.334, f32[3,16,64,127]{3,1,0,2:T(8,128)} %get-tuple-element.335, f32[3,16,64,127]{3,1,0,2:T(8,128)} %get-tuple-element.336, f32[3,16,64,1]{3,1,0,2:T(8,128)} %get-tuple-element.337, ...), kind=kLoop, calls=%fused_computation.9.clone.1 | loop fusion | flops 10223616 | bytes 14688640 | tf_op jit(solution)/shard_map/while/body/eval_jaxpr/mul | solution.py:102
  136.1 8.1 multiply_add_fusion.7
  148.5 9.5 %fusion.94 = f32[3,16,64,128]{3,1,0,2:T(8,128)} fusion(f32[3,16,64,128]{3,1,0,2:T(8,128)} %get-tuple-element.374, f32[3,16,64,1]{3,1,0,2:T(8,128)} %get-tuple-element.334, f32[3,16,64,127]{3,1,0,2:T(8,128)} %get-tuple-element.335, f32[3,16,64,127]{3,1,0,2:T(8,128)} %get-tuple-element.336, f32[3,16,64,1]{3,1,0,2:T(8,128)} %get-tuple-element.337, ...), kind=kLoop, calls=%fused_computation.9.clone.1 | loop fusion | flops 10223616 | bytes 14688640 | tf_op jit(solution)/shard_map/while/body/eval_jaxpr/mul | solution.py:102
  189.9 8.1 multiply_add_fusion.7
  202.3 9.5 %fusion.94 = f32[3,16,64,128]{3,1,0,2:T(8,128)} fusion(f32[3,16,64,128]{3,1,0,2:T(8,128)} %get-tuple-element.374, f32[3,16,64,1]{3,1,0,2:T(8,128)} %get-tuple-element.334, f32[3,16,64,127]{3,1,0,2:T(8,128)} %get-tuple-element.335, f32[3,16,64,127]{3,1,0,2:T(8,128)} %get-tuple-element.336, f32[3,16,64,1]{3,1,0,2:T(8,128)} %get-tuple-element.337, ...), kind=kLoop, calls=%fused_computation.9.clone.1 | loop fusion | flops 10223616 | bytes 14688640 | tf_op jit(solution)/shard_map/while/body/eval_jaxpr/mul | solution.py:102
  243.7 8.1 multiply_add_fusion.7
  256.1 9.5 %fusion.94 = f32[3,16,64,128]{3,1,0,2:T(8,128)} fusion(f32[3,16,64,128]{3,1,0,2:T(8,128)} %get-tuple-element.374, f32[3,16,64,1]{3,1,0,2:T(8,128)} %get-tuple-element.334, f32[3,16,64,127]{3,1,0,2:T(8,128)} %get-tuple-element.335, f32[3,16,64,127]{3,1,0,2:T(8,128)} %get-tuple-element.336, f32[3,16,64,1]{3,1,0,2:T(8,128)} %get-tuple-element.337, ...), kind=kLoop, calls=%fused_computation.9.clone.1 | loop fusion | flops 10223616 | bytes 14688640 | tf_op jit(solution)/shard_map/while/body/eval_jaxpr/mul | solution.py:102
  309.8 9.5 %fusion.94 = f32[3,16,64,128]{3,1,0,2:T(8,128)} fusion(f32[3,16,64,128]{3,1,0,2:T(8,128)} %get-tuple-element.374, f32[3,16,64,1]{3,1,0,2:T(8,128)} %get-tuple-element.334, f32[3,16,64,127]{3,1,0,2:T(8,128)} %get-tuple-element.335, f32[3,16,64,127]{3,1,0,2:T(8,128)} %get-tuple-element.336, f32[3,16,64,1]{3,1,0,2:T(8,128)} %get-tuple-element.337, ...), kind=kLoop, calls=%fused_computation.9.clone.1 | loop fusion | flops 10223616 | bytes 14688640 | tf_op jit(solution)/shard_map/while/body/eval_jaxpr/mul | solution.py:102
  351.2 8.1 multiply_add_fusion.7
  363.6 9.5 %fusion.94 = f32[3,16,64,128]{3,1,0,2:T(8,128)} fusion(f32[3,16,64,128]{3,1,0,2:T(8,128)} %get-tuple-element.374, f32[3,16,64,1]{3,1,0,2:T(8,128)} %get-tuple-element.334, f32[3,16,64,127]{3,1,0,2:T(8,128)} %get-tuple-element.335, f32[3,16,64,127]{3,1,0,2:T(8,128)} %get-tuple-element.336, f32[3,16,64,1]{3,1,0,2:T(8,128)} %get-tuple-element.337, ...), kind=kLoop, calls=%fused_computation.9.clone.1 | loop fusion | flops 10223616 | bytes 14688640 | tf_op jit(solution)/shard_map/while/body/eval_jaxpr/mul | solution.py:102
  417.4 9.5 %fusion.94 = f32[3,16,64,128]{3,1,0,2:T(8,128)} fusion(f32[3,16,64,128]{3,1,0,2:T(8,128)} %get-tuple-element.374, f32[3,16,64,1]{3,1,0,2:T(8,128)} %get-tuple-element.334, f32[3,16,64,127]{3,1,0,2:T(8,128)} %get-tuple-element.335, f32[3,16,64,127]{3,1,0,2:T(8,128)} %get-tuple-element.336, f32[3,16,64,1]{3,1,0,2:T(8,128)} %get-tuple-element.337, ...), kind=kLoop, calls=%fused_computation.9.clone.1 | loop fusion | flops 10223616 | bytes 14688640 | tf_op jit(solution)/shard_map/while/body/eval_jaxpr/mul | solution.py:102
  458.8 8.1 multiply_add_fusion.7
  471.1 9.5 %fusion.94 = f32[3,16,64,128]{3,1,0,2:T(8,128)} fusion(f32[3,16,64,128]{3,1,0,2:T(8,128)} %get-tuple-element.374, f32[3,16,64,1]{3,1,0,2:T(8,128)} %get-tuple-element.334, f32[3,16,64,127]{3,1,0,2:T(8,128)} %get-tuple-element.335, f32[3,16,64,127]{3,1,0,2:T(8,128)} %get-tuple-element.336, f32[3,16,64,1]{3,1,0,2:T(8,128)} %get-tuple-element.337, ...), kind=kLoop, calls=%fused_computation.9.clone.1 | loop fusion | flops 10223616 | bytes 14688640 | tf_op jit(solution)/shard_map/while/body/eval_jaxpr/mul | solution.py:102
  524.9 9.5 %fusion.94 = f32[3,16,64,128]{3,1,0,2:T(8,128)} fusion(f32[3,16,64,128]{3,1,0,2:T(8,128)} %get-tuple-element.374, f32[3,16,64,1]{3,1,0,2:T(8,128)} %get-tuple-element.334, f32[3,16,64,127]{3,1,0,2:T(8,128)} %get-tuple-element.335, f32[3,16,64,127]{3,1,0,2:T(8,128)} %get-tuple-element.336, f32[3,16,64,1]{3,1,0,2:T(8,128)} %get-tuple-element.337, ...), kind=kLoop, calls=%fused_computation.9.clone.1 | loop fusion | flops 10223616 | bytes 14688640 | tf_op jit(solution)/shard_map/while/body/eval_jaxpr/mul | solution.py:102
  578.7 9.5 %fusion.94 = f32[3,16,64,128]{3,1,0,2:T(8,128)} fusion(f32[3,16,64,128]{3,1,0,2:T(8,128)} %get-tuple-element.374, f32[3,16,64,1]{3,1,0,2:T(8,128)} %get-tuple-element.334, f32[3,16,64,127]{3,1,0,2:T(8,128)} %get-tuple-element.335, f32[3,16,64,127]{3,1,0,2:T(8,128)} %get-tuple-element.336, f32[3,16,64,1]{3,1,0,2:T(8,128)} %get-tuple-element.337, ...), kind=kLoop, calls=%fused_computation.9.clone.1 | loop fusion | flops 10223616 | bytes 14688640 | tf_op jit(solution)/shard_map/while/body/eval_jaxpr/mul | solution.py:102
  632.5 9.5 %fusion.94 = f32[3,16,64,128]{3,1,0,2:T(8,128)} fusion(f32[3,16,64,128]{3,1,0,2:T(8,128)} %get-tuple-element.374, f32[3,16,64,1]{3,1,0,2:T(8,128)} %get-tuple-element.334, f32[3,16,64,127]{3,1,0,2:T(8,128)} %get-tuple-element.335, f32[3,16,64,127]{3,1,0,2:T(8,128)} %get-tuple-element.336, f32[3,16,64,1]{3,1,0,2:T(8,128)} %get-tuple-element.337, ...), kind=kLoop, calls=%fused_computation.9.clone.1 | loop fusion | flops 10223616 | bytes 14688640 | tf_op jit(solution)/shard_map/while/body/eval_jaxpr/mul | solution.py:102
  686.2 9.5 %fusion.94 = f32[3,16,64,128]{3,1,0,2:T(8,128)} fusion(f32[3,16,64,128]{3,1,0,2:T(8,128)} %get-tuple-element.374, f32[3,16,64,1]{3,1,0,2:T(8,128)} %get-tuple-element.334, f32[3,16,64,127]{3,1,0,2:T(8,128)} %get-tuple-element.335, f32[3,16,64,127]{3,1,0,2:T(8,128)} %get-tuple-element.336, f32[3,16,64,1]{3,1,0,2:T(8,128)} %get-tuple-element.337, ...), kind=kLoop, calls=%fused_computation.9.clone.1 | loop fusion | flops 10223616 | bytes 14688640 | tf_op jit(solution)/shard_map/while/body/eval_jaxpr/mul | solution.py:102
  740.0 9.5 %fusion.94 = f32[3,16,64,128]{3,1,0,2:T(8,128)} fusion(f32[3,16,64,128]{3,1,0,2:T(8,128)} %get-tuple-element.374, f32[3,16,64,1]{3,1,0,2:T(8,128)} %get-tuple-element.334, f32[3,16,64,127]{3,1,0,2:T(8,128)} %get-tuple-element.335, f32[3,16,64,127]{3,1,0,2:T(8,128)} %get-tuple-element.336, f32[3,16,64,1]{3,1,0,2:T(8,128)} %get-tuple-element.337, ...), kind=kLoop, calls=%fused_computation.9.clone.1 | loop fusion | flops 10223616 | bytes 14688640 | tf_op jit(solution)/shard_map/while/body/eval_jaxpr/mul | solution.py:102
  793.8 9.5 %fusion.94 = f32[3,16,64,128]{3,1,0,2:T(8,128)} fusion(f32[3,16,64,128]{3,1,0,2:T(8,128)} %get-tuple-element.374, f32[3,16,64,1]{3,1,0,2:T(8,128)} %get-tuple-element.334, f32[3,16,64,127]{3,1,0,2:T(8,128)} %get-tuple-element.335, f32[3,16,64,127]{3,1,0,2:T(8,128)} %get-tuple-element.336, f32[3,16,64,1]{3,1,0,2:T(8,128)} %get-tuple-element.337, ...), kind=kLoop, calls=%fused_computation.9.clone.1 | loop fusion | flops 10223616 | bytes 14688640 | tf_op jit(solution)/shard_map/while/body/eval_jaxpr/mul | solution.py:102
  847.6 9.5 %fusion.94 = f32[3,16,64,128]{3,1,0,2:T(8,128)} fusion(f32[3,16,64,128]{3,1,0,2:T(8,128)} %get-tuple-element.374, f32[3,16,64,1]{3,1,0,2:T(8,128)} %get-tuple-element.334, f32[3,16,64,127]{3,1,0,2:T(8,128)} %get-tuple-element.335, f32[3,16,64,127]{3,1,0,2:T(8,128)} %get-tuple-element.336, f32[3,16,64,1]{3,1,0,2:T(8,128)} %get-tuple-element.337, ...), kind=kLoop, calls=%fused_computation.9.clone.1 | loop fusion | flops 10223616 | bytes 14688640 | tf_op jit(solution)/shard_map/while/body/eval_jaxpr/mul | solution.py:102
  883.2 8.5 multiply_add_fusion.5
  894.3 8.2 fusion.24
  (636 shorter events, 694.0 us)
Async XLA Ops:
  53.6 41.1 %collective-permute-start = (f32[1,3,16,128]{3,2,1,0:T(8,128)}, f32[1,3,16,128]{3,2,1,0:T(8,128)}, u32[]{:S(2)}, u32[]{:S(2)}) collective-permute-start(f32[1,3,16,128]{3,2,1,0:T(8,128)} %get-tuple-element.354), channel_id=1, source_target_pairs={{0,4},{4,8},{8,12},{1,5},{5,9},{9,13},{2,6},{6,10},{10,14},{3,7},{... | collective-permute-start | bytes 73736 | tf_op jit(solution)/shard_map/while/body/eval_jaxpr/ppermute | solution.py:17
  105.7 42.8 %collective-permute-start = (f32[1,3,16,128]{3,2,1,0:T(8,128)}, f32[1,3,16,128]{3,2,1,0:T(8,128)}, u32[]{:S(2)}, u32[]{:S(2)}) collective-permute-start(f32[1,3,16,128]{3,2,1,0:T(8,128)} %get-tuple-element.354), channel_id=1, source_target_pairs={{0,4},{4,8},{8,12},{1,5},{5,9},{9,13},{2,6},{6,10},{10,14},{3,7},{... | collective-permute-start | bytes 73736 | tf_op jit(solution)/shard_map/while/body/eval_jaxpr/ppermute | solution.py:17
  110.8 37.7 %collective-permute-start.1 = (f32[1,3,16,128]{3,2,1,0:T(8,128)}, f32[1,3,16,128]{3,2,1,0:T(8,128)}, u32[]{:S(2)}, u32[]{:S(2)}) collective-permute-start(f32[1,3,16,128]{3,2,1,0:T(8,128)} %get-tuple-element.355), channel_id=1, source_target_pairs={{4,0},{8,4},{12,8},{5,1},{9,5},{13,9},{6,2},{10,6},{14,10},{7,3},{... | collective-permute-start | bytes 73736 | tf_op jit(solution)/shard_map/while/body/eval_jaxpr/ppermute | solution.py:19
  159.4 42.8 %collective-permute-start = (f32[1,3,16,128]{3,2,1,0:T(8,128)}, f32[1,3,16,128]{3,2,1,0:T(8,128)}, u32[]{:S(2)}, u32[]{:S(2)}) collective-permute-start(f32[1,3,16,128]{3,2,1,0:T(8,128)} %get-tuple-element.354), channel_id=1, source_target_pairs={{0,4},{4,8},{8,12},{1,5},{5,9},{9,13},{2,6},{6,10},{10,14},{3,7},{... | collective-permute-start | bytes 73736 | tf_op jit(solution)/shard_map/while/body/eval_jaxpr/ppermute | solution.py:17
  164.6 37.7 %collective-permute-start.1 = (f32[1,3,16,128]{3,2,1,0:T(8,128)}, f32[1,3,16,128]{3,2,1,0:T(8,128)}, u32[]{:S(2)}, u32[]{:S(2)}) collective-permute-start(f32[1,3,16,128]{3,2,1,0:T(8,128)} %get-tuple-element.355), channel_id=1, source_target_pairs={{4,0},{8,4},{12,8},{5,1},{9,5},{13,9},{6,2},{10,6},{14,10},{7,3},{... | collective-permute-start | bytes 73736 | tf_op jit(solution)/shard_map/while/body/eval_jaxpr/ppermute | solution.py:19
  213.2 42.8 %collective-permute-start = (f32[1,3,16,128]{3,2,1,0:T(8,128)}, f32[1,3,16,128]{3,2,1,0:T(8,128)}, u32[]{:S(2)}, u32[]{:S(2)}) collective-permute-start(f32[1,3,16,128]{3,2,1,0:T(8,128)} %get-tuple-element.354), channel_id=1, source_target_pairs={{0,4},{4,8},{8,12},{1,5},{5,9},{9,13},{2,6},{6,10},{10,14},{3,7},{... | collective-permute-start | bytes 73736 | tf_op jit(solution)/shard_map/while/body/eval_jaxpr/ppermute | solution.py:17
  218.3 37.7 %collective-permute-start.1 = (f32[1,3,16,128]{3,2,1,0:T(8,128)}, f32[1,3,16,128]{3,2,1,0:T(8,128)}, u32[]{:S(2)}, u32[]{:S(2)}) collective-permute-start(f32[1,3,16,128]{3,2,1,0:T(8,128)} %get-tuple-element.355), channel_id=1, source_target_pairs={{4,0},{8,4},{12,8},{5,1},{9,5},{13,9},{6,2},{10,6},{14,10},{7,3},{... | collective-permute-start | bytes 73736 | tf_op jit(solution)/shard_map/while/body/eval_jaxpr/ppermute | solution.py:19
  267.0 42.8 %collective-permute-start = (f32[1,3,16,128]{3,2,1,0:T(8,128)}, f32[1,3,16,128]{3,2,1,0:T(8,128)}, u32[]{:S(2)}, u32[]{:S(2)}) collective-permute-start(f32[1,3,16,128]{3,2,1,0:T(8,128)} %get-tuple-element.354), channel_id=1, source_target_pairs={{0,4},{4,8},{8,12},{1,5},{5,9},{9,13},{2,6},{6,10},{10,14},{3,7},{... | collective-permute-start | bytes 73736 | tf_op jit(solution)/shard_map/while/body/eval_jaxpr/ppermute | solution.py:17
  272.1 37.7 %collective-permute-start.1 = (f32[1,3,16,128]{3,2,1,0:T(8,128)}, f32[1,3,16,128]{3,2,1,0:T(8,128)}, u32[]{:S(2)}, u32[]{:S(2)}) collective-permute-start(f32[1,3,16,128]{3,2,1,0:T(8,128)} %get-tuple-element.355), channel_id=1, source_target_pairs={{4,0},{8,4},{12,8},{5,1},{9,5},{13,9},{6,2},{10,6},{14,10},{7,3},{... | collective-permute-start | bytes 73736 | tf_op jit(solution)/shard_map/while/body/eval_jaxpr/ppermute | solution.py:19
  320.8 42.8 %collective-permute-start = (f32[1,3,16,128]{3,2,1,0:T(8,128)}, f32[1,3,16,128]{3,2,1,0:T(8,128)}, u32[]{:S(2)}, u32[]{:S(2)}) collective-permute-start(f32[1,3,16,128]{3,2,1,0:T(8,128)} %get-tuple-element.354), channel_id=1, source_target_pairs={{0,4},{4,8},{8,12},{1,5},{5,9},{9,13},{2,6},{6,10},{10,14},{3,7},{... | collective-permute-start | bytes 73736 | tf_op jit(solution)/shard_map/while/body/eval_jaxpr/ppermute | solution.py:17
  325.9 37.7 %collective-permute-start.1 = (f32[1,3,16,128]{3,2,1,0:T(8,128)}, f32[1,3,16,128]{3,2,1,0:T(8,128)}, u32[]{:S(2)}, u32[]{:S(2)}) collective-permute-start(f32[1,3,16,128]{3,2,1,0:T(8,128)} %get-tuple-element.355), channel_id=1, source_target_pairs={{4,0},{8,4},{12,8},{5,1},{9,5},{13,9},{6,2},{10,6},{14,10},{7,3},{... | collective-permute-start | bytes 73736 | tf_op jit(solution)/shard_map/while/body/eval_jaxpr/ppermute | solution.py:19
  374.5 42.8 %collective-permute-start = (f32[1,3,16,128]{3,2,1,0:T(8,128)}, f32[1,3,16,128]{3,2,1,0:T(8,128)}, u32[]{:S(2)}, u32[]{:S(2)}) collective-permute-start(f32[1,3,16,128]{3,2,1,0:T(8,128)} %get-tuple-element.354), channel_id=1, source_target_pairs={{0,4},{4,8},{8,12},{1,5},{5,9},{9,13},{2,6},{6,10},{10,14},{3,7},{... | collective-permute-start | bytes 73736 | tf_op jit(solution)/shard_map/while/body/eval_jaxpr/ppermute | solution.py:17
  379.7 37.7 %collective-permute-start.1 = (f32[1,3,16,128]{3,2,1,0:T(8,128)}, f32[1,3,16,128]{3,2,1,0:T(8,128)}, u32[]{:S(2)}, u32[]{:S(2)}) collective-permute-start(f32[1,3,16,128]{3,2,1,0:T(8,128)} %get-tuple-element.355), channel_id=1, source_target_pairs={{4,0},{8,4},{12,8},{5,1},{9,5},{13,9},{6,2},{10,6},{14,10},{7,3},{... | collective-permute-start | bytes 73736 | tf_op jit(solution)/shard_map/while/body/eval_jaxpr/ppermute | solution.py:19
  428.3 42.8 %collective-permute-start = (f32[1,3,16,128]{3,2,1,0:T(8,128)}, f32[1,3,16,128]{3,2,1,0:T(8,128)}, u32[]{:S(2)}, u32[]{:S(2)}) collective-permute-start(f32[1,3,16,128]{3,2,1,0:T(8,128)} %get-tuple-element.354), channel_id=1, source_target_pairs={{0,4},{4,8},{8,12},{1,5},{5,9},{9,13},{2,6},{6,10},{10,14},{3,7},{... | collective-permute-start | bytes 73736 | tf_op jit(solution)/shard_map/while/body/eval_jaxpr/ppermute | solution.py:17
  482.1 42.8 %collective-permute-start = (f32[1,3,16,128]{3,2,1,0:T(8,128)}, f32[1,3,16,128]{3,2,1,0:T(8,128)}, u32[]{:S(2)}, u32[]{:S(2)}) collective-permute-start(f32[1,3,16,128]{3,2,1,0:T(8,128)} %get-tuple-element.354), channel_id=1, source_target_pairs={{0,4},{4,8},{8,12},{1,5},{5,9},{9,13},{2,6},{6,10},{10,14},{3,7},{... | collective-permute-start | bytes 73736 | tf_op jit(solution)/shard_map/while/body/eval_jaxpr/ppermute | solution.py:17
  487.2 37.7 %collective-permute-start.1 = (f32[1,3,16,128]{3,2,1,0:T(8,128)}, f32[1,3,16,128]{3,2,1,0:T(8,128)}, u32[]{:S(2)}, u32[]{:S(2)}) collective-permute-start(f32[1,3,16,128]{3,2,1,0:T(8,128)} %get-tuple-element.355), channel_id=1, source_target_pairs={{4,0},{8,4},{12,8},{5,1},{9,5},{13,9},{6,2},{10,6},{14,10},{7,3},{... | collective-permute-start | bytes 73736 | tf_op jit(solution)/shard_map/while/body/eval_jaxpr/ppermute | solution.py:19
  535.8 42.8 %collective-permute-start = (f32[1,3,16,128]{3,2,1,0:T(8,128)}, f32[1,3,16,128]{3,2,1,0:T(8,128)}, u32[]{:S(2)}, u32[]{:S(2)}) collective-permute-start(f32[1,3,16,128]{3,2,1,0:T(8,128)} %get-tuple-element.354), channel_id=1, source_target_pairs={{0,4},{4,8},{8,12},{1,5},{5,9},{9,13},{2,6},{6,10},{10,14},{3,7},{... | collective-permute-start | bytes 73736 | tf_op jit(solution)/shard_map/while/body/eval_jaxpr/ppermute | solution.py:17
  589.6 42.8 %collective-permute-start = (f32[1,3,16,128]{3,2,1,0:T(8,128)}, f32[1,3,16,128]{3,2,1,0:T(8,128)}, u32[]{:S(2)}, u32[]{:S(2)}) collective-permute-start(f32[1,3,16,128]{3,2,1,0:T(8,128)} %get-tuple-element.354), channel_id=1, source_target_pairs={{0,4},{4,8},{8,12},{1,5},{5,9},{9,13},{2,6},{6,10},{10,14},{3,7},{... | collective-permute-start | bytes 73736 | tf_op jit(solution)/shard_map/while/body/eval_jaxpr/ppermute | solution.py:17
  643.4 42.8 %collective-permute-start = (f32[1,3,16,128]{3,2,1,0:T(8,128)}, f32[1,3,16,128]{3,2,1,0:T(8,128)}, u32[]{:S(2)}, u32[]{:S(2)}) collective-permute-start(f32[1,3,16,128]{3,2,1,0:T(8,128)} %get-tuple-element.354), channel_id=1, source_target_pairs={{0,4},{4,8},{8,12},{1,5},{5,9},{9,13},{2,6},{6,10},{10,14},{3,7},{... | collective-permute-start | bytes 73736 | tf_op jit(solution)/shard_map/while/body/eval_jaxpr/ppermute | solution.py:17
  648.5 37.7 %collective-permute-start.1 = (f32[1,3,16,128]{3,2,1,0:T(8,128)}, f32[1,3,16,128]{3,2,1,0:T(8,128)}, u32[]{:S(2)}, u32[]{:S(2)}) collective-permute-start(f32[1,3,16,128]{3,2,1,0:T(8,128)} %get-tuple-element.355), channel_id=1, source_target_pairs={{4,0},{8,4},{12,8},{5,1},{9,5},{13,9},{6,2},{10,6},{14,10},{7,3},{... | collective-permute-start | bytes 73736 | tf_op jit(solution)/shard_map/while/body/eval_jaxpr/ppermute | solution.py:19
  697.2 42.8 %collective-permute-start = (f32[1,3,16,128]{3,2,1,0:T(8,128)}, f32[1,3,16,128]{3,2,1,0:T(8,128)}, u32[]{:S(2)}, u32[]{:S(2)}) collective-permute-start(f32[1,3,16,128]{3,2,1,0:T(8,128)} %get-tuple-element.354), channel_id=1, source_target_pairs={{0,4},{4,8},{8,12},{1,5},{5,9},{9,13},{2,6},{6,10},{10,14},{3,7},{... | collective-permute-start | bytes 73736 | tf_op jit(solution)/shard_map/while/body/eval_jaxpr/ppermute | solution.py:17
  750.9 42.8 %collective-permute-start = (f32[1,3,16,128]{3,2,1,0:T(8,128)}, f32[1,3,16,128]{3,2,1,0:T(8,128)}, u32[]{:S(2)}, u32[]{:S(2)}) collective-permute-start(f32[1,3,16,128]{3,2,1,0:T(8,128)} %get-tuple-element.354), channel_id=1, source_target_pairs={{0,4},{4,8},{8,12},{1,5},{5,9},{9,13},{2,6},{6,10},{10,14},{3,7},{... | collective-permute-start | bytes 73736 | tf_op jit(solution)/shard_map/while/body/eval_jaxpr/ppermute | solution.py:17
  756.1 37.7 %collective-permute-start.1 = (f32[1,3,16,128]{3,2,1,0:T(8,128)}, f32[1,3,16,128]{3,2,1,0:T(8,128)}, u32[]{:S(2)}, u32[]{:S(2)}) collective-permute-start(f32[1,3,16,128]{3,2,1,0:T(8,128)} %get-tuple-element.355), channel_id=1, source_target_pairs={{4,0},{8,4},{12,8},{5,1},{9,5},{13,9},{6,2},{10,6},{14,10},{7,3},{... | collective-permute-start | bytes 73736 | tf_op jit(solution)/shard_map/while/body/eval_jaxpr/ppermute | solution.py:19
  804.7 42.8 %collective-permute-start = (f32[1,3,16,128]{3,2,1,0:T(8,128)}, f32[1,3,16,128]{3,2,1,0:T(8,128)}, u32[]{:S(2)}, u32[]{:S(2)}) collective-permute-start(f32[1,3,16,128]{3,2,1,0:T(8,128)} %get-tuple-element.354), channel_id=1, source_target_pairs={{0,4},{4,8},{8,12},{1,5},{5,9},{9,13},{2,6},{6,10},{10,14},{3,7},{... | collective-permute-start | bytes 73736 | tf_op jit(solution)/shard_map/while/body/eval_jaxpr/ppermute | solution.py:17
  (93 other events, 2339.0 us)
where the time goes:
time: 912 us; the launch traced here: 905 us
  other arithmetic  389 us (43%)
  local copies, waits for them, and re-layouts  346 us (38%)
  starting transfers between devices  163 us (18%)
    mul x16, other arithmetic, advance(): return ocean_plane * (adjoint + change + vert_change + coupled)  151 us
    add x16, other arithmetic, advance(): sum((reaction[source, tracer] * adjoint[source] for source in range(trace...  131 us
    ppermute x34, starting transfers between devices, padded(): lax.ppermute(tail, axis, [(i, (i + 1) % count) for i in range(ends)])  130 us
    slice x30, local copies, waits for them, and re-layouts, advance(): adjoint[:, :, :, -1]  91.1 us
    while x45, local copies, waits for them, and re-layouts  55.4 us
    mul x16, other arithmetic, advance(): vert_flux = vertical * (adjoint[:, 1:] - adjoint[:, :-1])  41 us
    slice x16, local copies, waits for them, and re-layouts, advance(): jnp.roll(adjoint, 1, axis=3)  34.8 us
    slice x16, local copies, waits for them, and re-layouts, advance(): adjoint[:, :, :, 0]  32.8 us
  transfers between devices with their start and end apart: 69, of which 0 were waited for; matrix products, arithmetic and copies ran while one was open for 61% of the time, Pallas kernels for 0%

commit v1 on v0

v1 whole, which is shorter than its diff:
```python
import functools

import jax
import jax.numpy as jnp
from jax import lax
from jax.experimental import pallas as pl
from jax.experimental.pallas import tpu as pltpu
from jax.sharding import PartitionSpec as P

NSTEP = 16
F32 = jnp.float32
MESH = pl.DeviceIdType.MESH
CHUNKS = 2
SUB = 8
LANES = 128


def ocean_kernel(
    shape,
    reaction,
    adjoint_end,
    east_flow,
    east_diff,
    north_flow,
    north_diff,
    vert_diff,
    ocean_mask,
    solubility,
    start_out,
    flux_out,
    state,
    c_east,
    c_west,
    c_north,
    c_south,
    c_zero,
    c_vert,
    ocean,
    total,
    raw,
    x_send,
    x_recv,
    y_send,
    y_recv,
    cx_send,
    cx_recv,
    cy_send,
    cy_recv,
    send_sem,
    recv_sem,
    coef_send_sem,
    coef_recv_sem,
):
    sections, bands, tiles = shape
    tracers, levels = adjoint_end.shape[:2]
    per_chunk = levels // CHUNKS
    pairs = per_chunk // 2
    sec, lat, lon = lax.axis_index("sec"), lax.axis_index("lat"), lax.axis_index("lon")
    ring = sections * tiles
    place = sec * tiles + lon
    east = lax.rem(place + 1, ring)
    west = lax.rem(place + ring - 1, ring)
    to_east = (lax.div(east, tiles), lat, lax.rem(east, tiles))
    to_west = (lax.div(west, tiles), lat, lax.rem(west, tiles))
    to_north = (sec, lax.min(lat + 1, bands - 1), lon)
    to_south = (sec, lax.max(lat - 1, 0), lon)
    has_north, has_south = lat < bands - 1, lat > 0

    lane = lax.broadcasted_iota(jnp.int32, (SUB, LANES), 1)
    sub = lax.broadcasted_iota(jnp.int32, (SUB, LANES), 0)
    first_lane, last_lane = lane == 0, lane == LANES - 1
    first_sub, last_sub = sub == 0, sub == SUB - 1
    even = lax.rem(lane, 2) == 0
    pair_of = lax.div(lane, 2)

    def pack(packed, value, j):
        moved = pltpu.roll(value, 2 * j + 1, 1)
        return moved if packed is None else jnp.where(pair_of == j, moved, packed)

    def merge(from_west, from_east):
        return jnp.where(even, pltpu.roll(from_east, LANES - 1, 1), pltpu.roll(from_west, 1, 1))

    def edge(merged, j):
        return pltpu.roll(merged, LANES - 2 * j - 1, 1)

    def northward(values, i, row):
        if i < SUB - 1:
            return values[i + 1]
        return jnp.where(last_sub, row, pltpu.roll(values[0], SUB - 1, 0))

    def southward(values, i, row):
        if i > 0:
            return values[i - 1]
        return jnp.where(first_sub, row, pltpu.roll(values[SUB - 1], 1, 0))

    def spread(row):
        return jnp.broadcast_to(row, (SUB, LANES))

    def coef_copies():
        out = []
        for d, (src, dst, dev) in enumerate(
            (
                (cx_send, cx_recv.at[0], to_east),
                (cx_send, cx_recv.at[1], to_west),
                (cy_send.at[0], cy_recv.at[0], to_north),
                (cy_send.at[1], cy_recv.at[1], to_south),
            )
        ):
            out.append(
                pltpu.make_async_remote_copy(
                    src_ref=src,
                    dst_ref=dst,
                    send_sem=coef_send_sem.at[d],
                    recv_sem=coef_recv_sem.at[d],
                    device_id=dev,
                    device_id_type=MESH,
                )
            )
        return out

    def copies(slot, g):
        out = []
        for d, (src, dst, dev) in enumerate(
            (
                (x_send.at[slot, g], x_recv.at[0, slot, g], to_east),
                (x_send.at[slot, g], x_recv.at[1, slot, g], to_west),
                (y_send.at[0, slot, g], y_recv.at[0, slot, g], to_north),
                (y_send.at[1, slot, g], y_recv.at[1, slot, g], to_south),
            )
        ):
            out.append(
                pltpu.make_async_remote_copy(
                    src_ref=src,
                    dst_ref=dst,
                    send_sem=send_sem.at[slot, g, d],
                    recv_sem=recv_sem.at[slot, g, d],
                    device_id=dev,
                    device_id_type=MESH,
                )
            )
        return out

    def start(c):
        c[0].start()
        c[1].start()
        pl.when(has_north)(c[2].start)
        pl.when(has_south)(c[3].start)

    def wait_send(c):
        c[0].wait_send()
        c[1].wait_send()
        pl.when(has_north)(c[2].wait_send)
        pl.when(has_south)(c[3].wait_send)

    def wait_recv(c):
        c[0].wait_recv()
        c[1].wait_recv()
        pl.when(has_south)(c[2].wait_recv)
        pl.when(has_north)(c[3].wait_recv)

    y_recv[...] = jnp.zeros_like(y_recv)
    cy_recv[...] = jnp.zeros_like(cy_recv)

    barrier = pltpu.get_barrier_semaphore()
    for dev in (to_east, to_west):
        pl.semaphore_signal(barrier, inc=1, device_id=dev, device_id_type=MESH)

    @pl.when(has_north)
    def _():
        pl.semaphore_signal(barrier, inc=1, device_id=to_north, device_id_type=MESH)

    @pl.when(has_south)
    def _():
        pl.semaphore_signal(barrier, inc=1, device_id=to_south, device_id_type=MESH)

    peers = 2 + has_north.astype(jnp.int32) + has_south.astype(jnp.int32)
    pl.semaphore_wait(barrier, peers)

    for i in range(SUB):
        ocean[i] = ocean_mask[pl.ds(i, SUB, stride=SUB), :].astype(F32)

    @pl.loop(0, levels)
    def _(l):
        flow, diff = east_flow[l].astype(F32), east_diff[l].astype(F32)
        raw[0] = 0.5 * flow + diff
        raw[1] = 0.5 * flow - diff
        flow, diff = north_flow[l].astype(F32), north_diff[l].astype(F32)
        raw[2] = 0.5 * flow + diff
        raw[3] = 0.5 * flow - diff
        packed = None
        for i in range(SUB):
            rows = pl.ds(i, SUB, stride=SUB)
            here = ocean[i]
            c_east[l, i] = raw[0, rows, :] * here
            back = raw[1, rows, :] * here
            c_west[l, i] = back
            packed = pack(packed, jnp.where(first_lane, here, back), i)
            c_north[l, i] = raw[2, rows, :] * here
            back = raw[3, rows, :] * here
            c_south[l, i] = back
            if i == SUB - 1:
                cy_send[0, pl.ds(l, 1), :] = back[SUB - 1 :, :]
            if i == 0:
                cy_send[1, pl.ds(l, 1), :] = here[:1, :]
        cx_send[l] = packed

    start(coef_copies())

    zero_plane = jnp.zeros((SUB, SUB, LANES), F32)
    for slot in range(2):
        for t in range(tracers):
            state[slot, t, 0] = zero_plane
            state[slot, t, levels + 1] = zero_plane
    c_vert[0] = zero_plane
    c_vert[levels] = zero_plane
    total[...] = jnp.zeros_like(total)

    def hand_over(slot, g, lp, dl, t, values, packed):
        row = lp * 2 + dl
        for i in range(SUB):
            packed = pack(packed, values[i], dl * tracers * SUB + t * SUB + i)
        y_send[0, slot, g, t, pl.ds(row, 1), :] = values[SUB - 1][SUB - 1 :, :]
        y_send[1, slot, g, t, pl.ds(row, 1), :] = values[0][:1, :]
        return packed

    for g in range(CHUNKS):

        @pl.loop(0, pairs)
        def _(lp):
            packed = None
            for dl in range(2):
                l = g * per_chunk + lp * 2 + dl
                for t in range(tracers):
                    values = []
                    for i in range(SUB):
                        cell = adjoint_end[t, l, pl.ds(i, SUB, stride=SUB), :] * ocean[i]
                        state[0, t, l + 1, i] = cell
                        values.append(cell)
                    packed = hand_over(0, g, lp, dl, t, values, packed)
            x_send[0, g, lp] = packed

        start(copies(0, g))

    @pl.loop(0, levels - 1)
    def _(l):
        raw[0] = vert_diff[l].astype(F32)
        for i in range(SUB):
            c_vert[l + 1, i] = raw[0, pl.ds(i, SUB, stride=SUB), :]

    wait_recv(coef_copies())

    @pl.loop(0, levels)
    def _(l):
        merged = merge(cx_recv[0, l], cx_recv[1, l])
        below = spread(cy_recv[0, pl.ds(l, 1), :])
        above = spread(cy_recv[1, pl.ds(l, 1), :])
        masks = [ocean[i] for i in range(SUB)]
        backs = [c_south[l, i] for i in range(SUB)]
        for i in range(SUB):
            here = masks[i]
            side = edge(merged, i)
            east_fwd = c_east[l, i] * jnp.where(last_lane, side, pltpu.roll(here, LANES - 1, 1))
            west_back = jnp.where(first_lane, side, pltpu.roll(c_west[l, i], 1, 1)) * here
            north_fwd = c_north[l, i] * northward(masks, i, above)
            south_back = southward(backs, i, below) * here
            c_east[l, i] = east_fwd
            c_west[l, i] = -west_back
            c_north[l, i] = north_fwd
            c_south[l, i] = -south_back
            c_zero[l, i] = (
                1.0
                - east_fwd
                + west_back
                - north_fwd
                + south_back
                - c_vert[l, i]
                - c_vert[l + 1, i]
            )

    wait_send(coef_copies())

    rate = [[reaction[s, t] for t in range(tracers)] for s in range(tracers)]

    @pl.loop(0, NSTEP)
    def _(k):
        now = lax.rem(k, 2)
        new = 1 - now
        for t in range(tracers):
            total[t] += state[now, t, 1]
        for g in range(CHUNKS):
            wait_recv(copies(now, g))

            @pl.when(k >= 1)
            def _():
                wait_send(copies(new, g))

            @pl.loop(0, pairs)
            def _(lp):
                merged = merge(x_recv[0, now, g, lp], x_recv[1, now, g, lp])
                packed = None
                for dl in range(2):
                    row = lp * 2 + dl
                    l = g * per_chunk + row
                    cells = [
                        [state[now, t, l + 1, i] for i in range(SUB)] for t in range(tracers)
                    ]
                    below = [
                        spread(y_recv[0, now, g, t, pl.ds(row, 1), :]) for t in range(tracers)
                    ]
                    above = [
                        spread(y_recv[1, now, g, t, pl.ds(row, 1), :]) for t in range(tracers)
                    ]
                    results = [[] for t in range(tracers)]
                    for i in range(SUB):
                        zero, vert_up, vert_down = c_zero[l, i], c_vert[l + 1, i], c_vert[l, i]
                        ce, cw, cn, cs = c_east[l, i], c_west[l, i], c_north[l, i], c_south[l, i]
                        for t in range(tracers):
                            a = cells[t][i]
                            side = edge(merged, dl * tracers * SUB + t * SUB + i)
                            value = (zero + rate[t][t]) * a
                            for s in range(tracers):
                                if s != t:
                                    value += rate[s][t] * cells[s][i]
                            value += vert_up * state[now, t, l + 2, i]
                            value += vert_down * state[now, t, l, i]
                            value += cn * northward(cells[t], i, above[t])
                            value += cs * southward(cells[t], i, below[t])
                            value += ce * jnp.where(last_lane, side, pltpu.roll(a, LANES - 1, 1))
                            value += cw * jnp.where(first_lane, side, pltpu.roll(a, 1, 1))
                            state[new, t, l + 1, i] = value
                            results[t].append(value)
                    for t in range(tracers):
                        packed = hand_over(new, g, lp, dl, t, results[t], packed)
                x_send[new, g, lp] = packed

            @pl.when(k < NSTEP - 1)
            def _():
                start(copies(new, g))

    for g in range(CHUNKS):
        wait_send(copies((NSTEP - 1) % 2, g))

    for i in range(SUB):
        rows = pl.ds(i, SUB, stride=SUB)
        acc = solubility[0, rows, :] * total[0, i]
        for t in range(1, tracers):
            acc += solubility[t, rows, :] * total[t, i]
        flux_out[rows, :] = ocean[i] * (acc * (1.0 / NSTEP))

    @pl.loop(0, levels)
    def _(l):
        for t in range(tracers):
            for i in range(SUB):
                start_out[t, l, pl.ds(i, SUB, stride=SUB), :] = state[NSTEP % 2, t, l + 1, i]


def run_ocean(shape, args, reaction):
    adjoint_end = args[0]
    tracers, levels, rows, cols = adjoint_end.shape
    per_chunk = levels // CHUNKS
    pairs = per_chunk // 2
    tile = (SUB, LANES)
    vmem = pl.BlockSpec(memory_space=pltpu.VMEM)
    coef = pltpu.VMEM((levels, SUB) + tile, F32)
    return pl.pallas_call(
        functools.partial(ocean_kernel, shape),
        out_shape=(
            jax.ShapeDtypeStruct(adjoint_end.shape, F32),
            jax.ShapeDtypeStruct((rows, cols), F32),
        ),
        in_specs=[pl.BlockSpec(memory_space=pltpu.SMEM)] + [vmem] * len(args),
        out_specs=(vmem, vmem),
        scratch_shapes=[
            pltpu.VMEM((2, tracers, levels + 2, SUB) + tile, F32),
            coef,
            coef,
            coef,
            coef,
            coef,
            pltpu.VMEM((levels + 1, SUB) + tile, F32),
            pltpu.VMEM((SUB,) + tile, F32),
            pltpu.VMEM((tracers, SUB) + tile, F32),
            pltpu.VMEM((4, rows, cols), F32),
            pltpu.VMEM((2, CHUNKS, pairs) + tile, F32),
            pltpu.VMEM((2, 2, CHUNKS, pairs) + tile, F32),
            pltpu.VMEM((2, 2, CHUNKS, tracers, per_chunk, cols), F32),
            pltpu.VMEM((2, 2, CHUNKS, tracers, per_chunk, cols), F32),
            pltpu.VMEM((levels,) + tile, F32),
            pltpu.VMEM((2, levels) + tile, F32),
            pltpu.VMEM((2, levels, cols), F32),
            pltpu.VMEM((2, levels, cols), F32),
            pltpu.SemaphoreType.DMA((2, CHUNKS, 4)),
            pltpu.SemaphoreType.DMA((2, CHUNKS, 4)),
            pltpu.SemaphoreType.DMA((4,)),
            pltpu.SemaphoreType.DMA((4,)),
        ],
        compiler_params=pltpu.CompilerParams(
            collective_id=0, has_side_effects=True, vmem_limit_bytes=48 * 1024 * 1024
        ),
    )(reaction, *args)


def exclusive_rank(hot, axis):
    count = hot.shape[axis]
    before = (jnp.arange(count)[:, None] < jnp.arange(count)[None, :]).astype(F32)
    return jnp.moveaxis(jnp.tensordot(hot, before, axes=((axis,), (0,))), -1, axis)


def deliver(blocks, route_tile, route_block, atm_rows):
    senders = lax.axis_size(("sec", "lon"))
    own_index = lax.axis_index(("sec", "lon"))
    block_count = blocks.shape[0]
    cell_count = blocks.shape[1]
    capacity = max(2, 2 * block_count // senders)
    dest_tiles = route_tile[:, :, 0]
    peer_ids = jnp.arange(senders, dtype=jnp.int32)
    slot_ids = jnp.arange(capacity, dtype=jnp.int32).astype(F32)
    own_tiles = lax.dynamic_index_in_dim(dest_tiles, own_index, 0, keepdims=False)
    dest_hot = (own_tiles[:, None] == peer_ids[None, :]).astype(F32)
    order_rank = exclusive_rank(dest_hot, 0)
    slot_index = jnp.sum(order_rank * dest_hot, axis=1)
    slot_hot = (slot_index[:, None] == slot_ids[None, :]).astype(F32)
    selector = (dest_hot[:, :, None] * slot_hot[:, None, :]).reshape(
        block_count, senders * capacity
    )
    outgoing = jnp.dot(selector.T, blocks, precision=lax.Precision.HIGHEST).reshape(
        senders, capacity, cell_count
    )
    incoming = lax.all_to_all(outgoing, ("sec", "lon"), split_axis=0, concat_axis=0, tiled=True)
    arrived = (dest_tiles == own_index).astype(F32)
    arrival_rank = exclusive_rank(arrived, 1)
    slot_take = arrived[:, :, None] * (arrival_rank[:, :, None] == slot_ids[None, None, :]).astype(
        F32
    )
    block_hot = (
        route_block[:, :, None] == jnp.arange(atm_rows, dtype=jnp.int32)[None, None, :]
    ).astype(F32)
    placing = jnp.einsum("syc,sya->asc", slot_take, block_hot, precision=lax.Precision.HIGHEST)
    placing = placing.reshape(atm_rows, senders * capacity)
    return jnp.dot(
        placing, incoming.reshape(senders * capacity, cell_count), precision=lax.Precision.HIGHEST
    )


def per_device(
    shape,
    adjoint_end,
    east_flow,
    east_diff,
    north_flow,
    north_diff,
    vert_diff,
    ocean_mask,
    reaction,
    solubility,
    route_tile,
    route_block,
    xgrid_weights,
    deposition,
):
    adjoint_start, flux = run_ocean(
        shape,
        (
            adjoint_end,
            east_flow,
            east_diff,
            north_flow,
            north_diff,
            vert_diff,
            ocean_mask,
            solubility,
        ),
        reaction,
    )
    blocks = jnp.einsum(
        "bo,boa->ba", flux.astype(jnp.bfloat16), xgrid_weights, preferred_element_type=F32
    )
    flux_adjoint = deliver(blocks, route_tile, route_block, deposition.shape[1])
    ash_adjoint = deposition.astype(F32) * flux_adjoint[None]
    return (adjoint_start, flux_adjoint, ash_adjoint)


def solution(mesh):
    shape = (mesh.shape["sec"], mesh.shape["lat"], mesh.shape["lon"])
    field = P(None, "lat", ("sec", "lon"))
    in_specs = (
        P(None, None, "lat", ("sec", "lon")),
        field,
        field,
        field,
        field,
        field,
        P("lat", ("sec", "lon")),
        P(),
        field,
        P(None, "lat", None),
        P(None, "lat"),
        P("lat", ("sec", "lon"), None),
        field,
    )
    out_specs = (
        P(None, None, "lat", ("sec", "lon")),
        P("lat", ("sec", "lon")),
        field,
    )
    return jax.shard_map(
        functools.partial(per_device, shape),
        mesh=mesh,
        in_specs=in_specs,
        out_specs=out_specs,
        check_vma=False,
    )
```

time: 912 us -> 139 us (0.15)
  other arithmetic: 389 us -> 0.96 us
  local copies, waits for them, and re-layouts: 346 us -> 13.2 us
  starting transfers between devices: 163 us -> 3.35 us
  Pallas kernels: 0 us -> 114 us
    slice x138 -> x0, local copies, waits for them, and re-layouts: 214 us -> none  [the longest x30 91.1 us: advance(): adjoint[:, :, :, -1]]
    mul x39 -> x1, other arithmetic: 197 us -> 0.86 us  [per_device(): ash_adjoint = deposition.astype(F32) * flux_adjoint[None]]
    ppermute x68 -> x0, starting transfers between devices: 159 us -> none  [the longest x34 130 us: padded(): lax.ppermute(tail, axis, [(i, (i + 1) % count) for i in range(ends)])]
    add x32 -> x0, other arithmetic: 147 us -> none  [the longest x16 131 us: advance(): sum((reaction[source, tracer] * adjoint[source] for source in range(trace...]
    pallas_call x0 -> x1, Pallas kernels: none -> 114 us  [run_ocean(): pl.pallas_call(functools.partial(ocean_kernel, shape), out_shape=(jax.Sha...]
    while x47 -> x0, local copies, waits for them, and re-layouts: 57.9 us -> none
    broadcast_in_dim x62 -> x0, local copies, waits for them, and re-layouts: 25.9 us -> none  [the longest x31 23.1 us: advance(): jnp.where(last_col, right[..., None], jnp.roll(adjoint, -1, axis=3))]
    ppermute x32 -> x0, other arithmetic: 21.6 us -> none  [the longest x16 10.8 us: padded(): lax.ppermute(tail, axis, [(i, (i + 1) % count) for i in range(ends)])]
  transfers between devices with their start and end apart: 69 -> 1, of which waited for: 0 -> 1; matrix products, arithmetic and copies ran while one was open for 61% -> 1% of each run, Pallas kernels for 0% -> 0%
where the time goes in v1:
time: 139 us
  Pallas kernels  114 us (82%)
  local copies, waits for them, and re-layouts  13.2 us (9%)
  waiting for transfers between devices  4.08 us (3%)
  starting transfers between devices  3.35 us (2%)
  matrix products  2.57 us (2%)
    pallas_call x1, Pallas kernels, run_ocean(): pl.pallas_call(functools.partial(ocean_kernel, shape), out_shape=(jax.Sha...  114 us
    unnamed x31, local copies, waits for them, and re-layouts  12.4 us
    all_to_all x1, waiting for transfers between devices, deliver(): lax.all_to_all(outgoing, ('sec', 'lon'), split_axis=0, concat_axis=0, til...  4.08 us
    all_to_all x1, starting transfers between devices, deliver(): lax.all_to_all(outgoing, ('sec', 'lon'), split_axis=0, concat_axis=0, til...  3.35 us
  transfers between devices with their start and end apart: 1, of which 1 were waited for; matrix products, arithmetic and copies ran while one was open for 1% of the time, Pallas kernels for 0%

profile of v1, /device:TPU:0, one launch (start us, length us, event | category | flops | bytes accessed | tf_op | source)
XLA Modules:
  0.0 138.6 jit_solution(3852862460598986852)
XLA Ops:
  0.7 0.8 dynamic-slice_bitcast_fusion
  1.5 0.1 fusion
  1.6 1.4 %copy-done.1 = f32[3,16,64,128]{3,2,1,0:T(8,128)S(1)} copy-done((f32[3,16,64,128]{3,2,1,0:T(8,128)S(1)}, f32[3,16,64,128]{3,2,1,0:T(8,128)}, u32[]{:S(2)}) %copy-start.1) | copy-done | bytes 1572888
  3.0 0.9 copy-done.3
  4.0 0.9 copy-done.4
  4.9 0.9 copy-done.5
  5.9 0.9 copy-done.6
  6.8 0.9 copy-done.7
  7.8 0.9 copy-done.8
  8.7 0.8 copy-done.9
  9.4 0.7 copy-done.10
  10.1 113.7 %shard_map.148 = (f32[3,16,64,128]{3,2,1,0:T(8,128)S(1)}, f32[64,128]{1,0:T(8,128)S(1)}) custom-call(f32[3,3]{1,0:T(4,128)S(1)} %copy-done.10, f32[3,16,64,128]{3,2,1,0:T(8,128)S(1)} %copy-done.1, bf16[16,64,128]{2,1,0:T(8,128)(2,1)S(1)} %copy-done.3, bf16[16,64,128]{2,1,0:T(8,128)(2,1)S(1)} %copy-done.4, bf16[16,64,128]{2,1,0:T(8,128)(2,1)S(1)} %copy-done.5, ...), custom_call_target="tpu_custom_call" | custom-call | tf_op jit(solution)/shard_map/pallas_call | solution.py:365
  123.8 1.2 copy-done.2
  125.0 0.6 fusion.11
  125.6 0.1 compare_convert_fusion
  125.7 0.8 fusion.8
  126.5 3.4 %all-to-all-start = ((f32[8,16,128]{2,1,0:T(8,128)}), f32[8,16,128]{2,1,0:T(8,128)S(1)}, u32[]{:S(2)}, u32[]{:S(2)}) async-start(f32[8,16,128]{2,1,0:T(8,128)} %fusion.8), calls=%async_computation | async-start | bytes 131072 | tf_op jit(solution)/shard_map/all_to_all | solution.py:429
  129.9 0.1 fusion.15
  130.1 0.6 convolution_bitcast_fusion
  130.7 4.1 %all-to-all-done = f32[8,16,128]{2,1,0:T(8,128)S(1)} async-done(((f32[8,16,128]{2,1,0:T(8,128)}), f32[8,16,128]{2,1,0:T(8,128)S(1)}, u32[]{:S(2)}, u32[]{:S(2)}) %all-to-all-start) | async-done | bytes 65568 | tf_op jit(solution)/shard_map/all_to_all | solution.py:429
  134.8 0.2 convolution_bitcast_fusion.1
  135.0 0.0 copy-done.11
  135.0 0.9 convert_multiply_fusion
  135.9 2.7 %copy.24 = f32[3,16,64,128]{3,2,1,0:T(8,128)} copy(f32[3,16,64,128]{3,2,1,0:T(8,128)} %copy-done.2) | data formatting | bytes 3145728
  (24 shorter events, 0.1 us)
Async XLA Ops:
  0.6 124.4 %copy-start = (bf16[64,128,128]{2,1,0:T(8,128)(2,1)S(1)}, bf16[64,128,128]{2,1,0:T(8,128)(2,1)}, u32[]{:S(2)}) copy-start(bf16[64,128,128]{2,1,0:T(8,128)(2,1)} %param.24) | copy-start | bytes 6291460
  1.6 1.4 %copy-start.1 = (f32[3,16,64,128]{3,2,1,0:T(8,128)S(1)}, f32[3,16,64,128]{3,2,1,0:T(8,128)}, u32[]{:S(2)}) copy-start(f32[3,16,64,128]{3,2,1,0:T(8,128)} %adjoint_end.1) | copy-start | bytes 4718596
  3.0 0.9 copy-start.3
  4.0 0.9 copy-start.4
  4.9 0.9 copy-start.5
  5.9 0.9 copy-start.6
  6.8 0.9 copy-start.7
  7.8 0.9 copy-start.8
  8.7 0.8 copy-start.9
  9.4 0.7 copy-start.10
  10.1 119.8 %copy-start.13 = (s32[8,64,1]{1,2,0:T(1,128)S(1)}, s32[8,64,1]{1,2,0:T(1,128)}, u32[]{:S(2)}) copy-start(s32[8,64,1]{1,2,0:T(1,128)} %param.22) | copy-start | bytes 6148
  10.1 120.0 %copy-start.14 = (s32[8,64]{1,0:T(8,128)S(1)}, s32[8,64]{1,0:T(8,128)}, u32[]{:S(2)}) copy-start(s32[8,64]{1,0:T(8,128)} %param.23) | copy-start | bytes 6148
  123.8 1.2 copy-start.2
  125.0 10.0 %copy-start.11 = (bf16[32,32,128]{2,1,0:T(8,128)(2,1)S(1)}, bf16[32,32,128]{2,1,0:T(8,128)(2,1)}, u32[]{:S(2)}) copy-start(bf16[32,32,128]{2,1,0:T(8,128)(2,1)} %param.25) | copy-start | bytes 786436
  126.5 8.2 %all-to-all-start = ((f32[8,16,128]{2,1,0:T(8,128)}), f32[8,16,128]{2,1,0:T(8,128)S(1)}, u32[]{:S(2)}, u32[]{:S(2)}) async-start(f32[8,16,128]{2,1,0:T(8,128)} %fusion.8), calls=%async_computation | async-start | bytes 131072 | tf_op jit(solution)/shard_map/all_to_all | solution.py:429
  135.0 3.6 %copy-start.12 = (f32[32,128]{1,0:T(8,128)}, f32[32,128]{1,0:T(8,128)S(1)}, u32[]{:S(2)}) copy-start(f32[32,128]{1,0:T(8,128)S(1)} %convolution_bitcast_fusion.1) | copy-start | bytes 49156

commit v2 on v1

--- a/solution.py
+++ b/solution.py
@@ -10,7 +10,7 @@
 NSTEP = 16
 F32 = jnp.float32
 MESH = pl.DeviceIdType.MESH
-CHUNKS = 2
+CHUNKS = 4
 SUB = 8
 LANES = 128
 
@@ -18,6 +18,16 @@
 def ocean_kernel(
     shape,
     reaction,
+    adjoint_end_in,
+    east_flow_in,
+    east_diff_in,
+    north_flow_in,
+    north_diff_in,
+    vert_diff_in,
+    ocean_mask_in,
+    solubility_in,
+    start_out,
+    flux_out,
     adjoint_end,
     east_flow,
     east_diff,
@@ -26,9 +36,8 @@
     vert_diff,
     ocean_mask,
     solubility,
-    start_out,
-    flux_out,
-    state,
+    state_even,
+    state_odd,
     c_east,
     c_west,
     c_north,
@@ -50,6 +59,7 @@
     recv_sem,
     coef_send_sem,
     coef_recv_sem,
+    load_sem,
 ):
     sections, bands, tiles = shape
     tracers, levels = adjoint_end.shape[:2]
@@ -158,6 +168,22 @@
         pl.when(has_south)(c[2].wait_recv)
         pl.when(has_north)(c[3].wait_recv)
 
+    loads = {}
+    for n, (src, dst) in enumerate(
+        (
+            (ocean_mask_in, ocean_mask),
+            (east_flow_in, east_flow),
+            (east_diff_in, east_diff),
+            (north_flow_in, north_flow),
+            (north_diff_in, north_diff),
+            (adjoint_end_in, adjoint_end),
+            (vert_diff_in, vert_diff),
+            (solubility_in, solubility),
+        )
+    ):
+        loads[n] = pltpu.make_async_copy(src, dst, load_sem.at[n])
+        loads[n].start()
+
     y_recv[...] = jnp.zeros_like(y_recv)
     cy_recv[...] = jnp.zeros_like(cy_recv)
 
@@ -176,6 +202,8 @@
     peers = 2 + has_north.astype(jnp.int32) + has_south.astype(jnp.int32)
     pl.semaphore_wait(barrier, peers)
 
+    for n in range(5):
+        loads[n].wait()
     for i in range(SUB):
         ocean[i] = ocean_mask[pl.ds(i, SUB, stride=SUB), :].astype(F32)
 
@@ -207,10 +235,10 @@
     start(coef_copies())
 
     zero_plane = jnp.zeros((SUB, SUB, LANES), F32)
-    for slot in range(2):
+    for state in (state_even, state_odd):
         for t in range(tracers):
-            state[slot, t, 0] = zero_plane
-            state[slot, t, levels + 1] = zero_plane
+            state[t, 0] = zero_plane
+            state[t, levels + 1] = zero_plane
     c_vert[0] = zero_plane
     c_vert[levels] = zero_plane
     total[...] = jnp.zeros_like(total)
@@ -223,6 +251,7 @@
         y_send[1, slot, g, t, pl.ds(row, 1), :] = values[0][:1, :]
         return packed
 
+    loads[5].wait()
     for g in range(CHUNKS):
 
         @pl.loop(0, pairs)
@@ -234,12 +263,14 @@
                     values = []
                     for i in range(SUB):
                         cell = adjoint_end[t, l, pl.ds(i, SUB, stride=SUB), :] * ocean[i]
-                        state[0, t, l + 1, i] = cell
+                        state_even[t, l + 1, i] = cell
                         values.append(cell)
                     packed = hand_over(0, g, lp, dl, t, values, packed)
             x_send[0, g, lp] = packed
 
         start(copies(0, g))
+
+    loads[6].wait()
 
     @pl.loop(0, levels - 1)
     def _(l):
@@ -281,16 +312,14 @@
 
     rate = [[reaction[s, t] for t in range(tracers)] for s in range(tracers)]
 
-    @pl.loop(0, NSTEP)
-    def _(k):
-        now = lax.rem(k, 2)
+    def step(now, old, fresh, must_wait, must_send):
         new = 1 - now
         for t in range(tracers):
-            total[t] += state[now, t, 1]
+            total[t] += old[t, 1]
         for g in range(CHUNKS):
             wait_recv(copies(now, g))
 
-            @pl.when(k >= 1)
+            @pl.when(must_wait)
             def _():
                 wait_send(copies(new, g))
 
@@ -301,45 +330,51 @@
                 for dl in range(2):
                     row = lp * 2 + dl
                     l = g * per_chunk + row
-                    cells = [
-                        [state[now, t, l + 1, i] for i in range(SUB)] for t in range(tracers)
-                    ]
+                    cells = [[old[t, l + 1, i] for i in range(SUB)] for t in range(tracers)]
                     below = [
                         spread(y_recv[0, now, g, t, pl.ds(row, 1), :]) for t in range(tracers)
                     ]
                     above = [
                         spread(y_recv[1, now, g, t, pl.ds(row, 1), :]) for t in range(tracers)
                     ]
-                    results = [[] for t in range(tracers)]
                     for i in range(SUB):
                         zero, vert_up, vert_down = c_zero[l, i], c_vert[l + 1, i], c_vert[l, i]
                         ce, cw, cn, cs = c_east[l, i], c_west[l, i], c_north[l, i], c_south[l, i]
                         for t in range(tracers):
                             a = cells[t][i]
-                            side = edge(merged, dl * tracers * SUB + t * SUB + i)
-                            value = (zero + rate[t][t]) * a
+                            j = dl * tracers * SUB + t * SUB + i
+                            side = edge(merged, j)
+                            own = (zero + rate[t][t]) * a
                             for s in range(tracers):
                                 if s != t:
-                                    value += rate[s][t] * cells[s][i]
-                            value += vert_up * state[now, t, l + 2, i]
-                            value += vert_down * state[now, t, l, i]
-                            value += cn * northward(cells[t], i, above[t])
-                            value += cs * southward(cells[t], i, below[t])
-                            value += ce * jnp.where(last_lane, side, pltpu.roll(a, LANES - 1, 1))
-                            value += cw * jnp.where(first_lane, side, pltpu.roll(a, 1, 1))
-                            state[new, t, l + 1, i] = value
-                            results[t].append(value)
-                    for t in range(tracers):
-                        packed = hand_over(new, g, lp, dl, t, results[t], packed)
+                                    own += rate[s][t] * cells[s][i]
+                            vert = vert_up * old[t, l + 2, i] + vert_down * old[t, l, i]
+                            meridian = cn * northward(cells[t], i, above[t])
+                            meridian += cs * southward(cells[t], i, below[t])
+                            zonal = ce * jnp.where(last_lane, side, pltpu.roll(a, LANES - 1, 1))
+                            zonal += cw * jnp.where(first_lane, side, pltpu.roll(a, 1, 1))
+                            value = (own + vert) + (meridian + zonal)
+                            fresh[t, l + 1, i] = value
+                            packed = pack(packed, value, j)
+                            if i == SUB - 1:
+                                y_send[0, new, g, t, pl.ds(row, 1), :] = value[SUB - 1 :, :]
+                            if i == 0:
+                                y_send[1, new, g, t, pl.ds(row, 1), :] = value[:1, :]
                 x_send[new, g, lp] = packed
 
-            @pl.when(k < NSTEP - 1)
+            @pl.when(must_send)
             def _():
                 start(copies(new, g))
 
+    @pl.loop(0, NSTEP // 2)
+    def _(k):
+        step(0, state_even, state_odd, k >= 1, k >= 0)
+        step(1, state_odd, state_even, k >= 0, k < NSTEP // 2 - 1)
+
     for g in range(CHUNKS):
         wait_send(copies((NSTEP - 1) % 2, g))
 
+    loads[7].wait()
     for i in range(SUB):
         rows = pl.ds(i, SUB, stride=SUB)
         acc = solubility[0, rows, :] * total[0, i]
@@ -351,7 +386,7 @@
     def _(l):
         for t in range(tracers):
             for i in range(SUB):
-                start_out[t, l, pl.ds(i, SUB, stride=SUB), :] = state[NSTEP % 2, t, l + 1, i]
+                start_out[t, l, pl.ds(i, SUB, stride=SUB), :] = state_even[t, l + 1, i]
 
 
 def run_ocean(shape, args, reaction):
@@ -368,10 +403,12 @@
             jax.ShapeDtypeStruct(adjoint_end.shape, F32),
             jax.ShapeDtypeStruct((rows, cols), F32),
         ),
-        in_specs=[pl.BlockSpec(memory_space=pltpu.SMEM)] + [vmem] * len(args),
+        in_specs=[pl.BlockSpec(memory_space=pltpu.SMEM)] + [pl.BlockSpec(memory_space=pl.ANY)] * len(args),
         out_specs=(vmem, vmem),
         scratch_shapes=[
-            pltpu.VMEM((2, tracers, levels + 2, SUB) + tile, F32),
+            *[pltpu.VMEM(arg.shape, arg.dtype) for arg in args],
+            pltpu.VMEM((tracers, levels + 2, SUB) + tile, F32),
+            pltpu.VMEM((tracers, levels + 2, SUB) + tile, F32),
             coef,
             coef,
             coef,
@@ -393,6 +430,7 @@
             pltpu.SemaphoreType.DMA((2, CHUNKS, 4)),
             pltpu.SemaphoreType.DMA((4,)),
             pltpu.SemaphoreType.DMA((4,)),
+            pltpu.SemaphoreType.DMA((len(args),)),
         ],
         compiler_params=pltpu.CompilerParams(
             collective_id=0, has_side_effects=True, vmem_limit_bytes=48 * 1024 * 1024

time: 139 us -> 104 us (0.75)
  Pallas kernels: 114 us -> 78.5 us
    pallas_call x1, Pallas kernels: 114 us -> 78.5 us  [run_ocean(): pl.pallas_call(functools.partial(ocean_kernel, shape), out_shape=(jax.Sha...]
where the time goes in v2:
time: 104 us; the launch traced here: 103 us
  Pallas kernels  78.5 us (75%)
  local copies, waits for them, and re-layouts  13.2 us (13%)
  waiting for transfers between devices  4.08 us (4%)
  starting transfers between devices  3.35 us (3%)
  matrix products  2.57 us (2%)
    pallas_call x1, Pallas kernels, run_ocean(): pl.pallas_call(functools.partial(ocean_kernel, shape), out_shape=(jax.Sha...  78.5 us
    unnamed x31, local copies, waits for them, and re-layouts  12.4 us
    all_to_all x1, waiting for transfers between devices, deliver(): lax.all_to_all(outgoing, ('sec', 'lon'), split_axis=0, concat_axis=0, til...  4.08 us
    all_to_all x1, starting transfers between devices, deliver(): lax.all_to_all(outgoing, ('sec', 'lon'), split_axis=0, concat_axis=0, til...  3.35 us
  transfers between devices with their start and end apart: 1, of which 1 were waited for; matrix products, arithmetic and copies ran while one was open for 1% of the time, Pallas kernels for 0%

profile of v2, /device:TPU:0, one launch (start us, length us, event | category | flops | bytes accessed | tf_op | source)
XLA Modules:
  0.0 103.5 jit_solution(13963773193873425880)
XLA Ops:
  0.7 0.8 dynamic-slice_bitcast_fusion
  1.5 0.1 fusion
  1.6 1.4 %copy-done.1 = f32[3,16,64,128]{3,2,1,0:T(8,128)S(1)} copy-done((f32[3,16,64,128]{3,2,1,0:T(8,128)S(1)}, f32[3,16,64,128]{3,2,1,0:T(8,128)}, u32[]{:S(2)}) %copy-start.1) | copy-done | bytes 1572888
  3.0 0.9 copy-done.3
  4.0 0.9 copy-done.4
  4.9 0.9 copy-done.5
  5.9 0.9 copy-done.6
  6.8 0.9 copy-done.7
  7.8 0.9 copy-done.8
  8.7 0.8 copy-done.9
  9.4 0.7 copy-done.10
  10.1 78.5 %shard_map.148 = (f32[3,16,64,128]{3,2,1,0:T(8,128)S(1)}, f32[64,128]{1,0:T(8,128)S(1)}) custom-call(f32[3,3]{1,0:T(4,128)S(1)} %copy-done.10, f32[3,16,64,128]{3,2,1,0:T(8,128)S(1)} %copy-done.1, bf16[16,64,128]{2,1,0:T(8,128)(2,1)S(1)} %copy-done.3, bf16[16,64,128]{2,1,0:T(8,128)(2,1)S(1)} %copy-done.4, bf16[16,64,128]{2,1,0:T(8,128)(2,1)S(1)} %copy-done.5, ...), custom_call_target="tpu_custom_call" | custom-call | tf_op jit(solution)/shard_map/pallas_call | solution.py:400
  88.7 1.2 %copy-done.2 = f32[3,16,64,128]{3,2,1,0:T(8,128)} copy-done((f32[3,16,64,128]{3,2,1,0:T(8,128)}, f32[3,16,64,128]{3,2,1,0:T(8,128)S(1)}, u32[]{:S(2)}) %copy-start.2) | copy-done | bytes 1572888
  89.9 0.6 fusion.11
  90.5 0.1 compare_convert_fusion
  90.6 0.8 fusion.8
  91.4 3.4 %all-to-all-start = ((f32[8,16,128]{2,1,0:T(8,128)}), f32[8,16,128]{2,1,0:T(8,128)S(1)}, u32[]{:S(2)}, u32[]{:S(2)}) async-start(f32[8,16,128]{2,1,0:T(8,128)} %fusion.8), calls=%async_computation | async-start | bytes 131072 | tf_op jit(solution)/shard_map/all_to_all | solution.py:467
  94.8 0.1 fusion.15
  94.9 0.6 convolution_bitcast_fusion
  95.5 4.1 %all-to-all-done = f32[8,16,128]{2,1,0:T(8,128)S(1)} async-done(((f32[8,16,128]{2,1,0:T(8,128)}), f32[8,16,128]{2,1,0:T(8,128)S(1)}, u32[]{:S(2)}, u32[]{:S(2)}) %all-to-all-start) | async-done | bytes 65568 | tf_op jit(solution)/shard_map/all_to_all | solution.py:467
  99.6 0.2 convolution_bitcast_fusion.1
  99.8 0.0 copy-done.11
  99.9 0.9 convert_multiply_fusion
  100.8 2.7 %copy.24 = f32[3,16,64,128]{3,2,1,0:T(8,128)} copy(f32[3,16,64,128]{3,2,1,0:T(8,128)} %copy-done.2) | data formatting | bytes 3145728
  (24 shorter events, 0.1 us)
Async XLA Ops:
  0.6 89.2 %copy-start = (bf16[64,128,128]{2,1,0:T(8,128)(2,1)S(1)}, bf16[64,128,128]{2,1,0:T(8,128)(2,1)}, u32[]{:S(2)}) copy-start(bf16[64,128,128]{2,1,0:T(8,128)(2,1)} %param.24) | copy-start | bytes 6291460
  1.6 1.4 %copy-start.1 = (f32[3,16,64,128]{3,2,1,0:T(8,128)S(1)}, f32[3,16,64,128]{3,2,1,0:T(8,128)}, u32[]{:S(2)}) copy-start(f32[3,16,64,128]{3,2,1,0:T(8,128)} %adjoint_end_in.1) | copy-start | bytes 4718596
  3.0 0.9 copy-start.3
  4.0 0.9 copy-start.4
  4.9 0.9 copy-start.5
  5.9 0.9 copy-start.6
  6.8 0.9 copy-start.7
  7.8 0.9 copy-start.8
  8.7 0.8 copy-start.9
  9.4 0.7 copy-start.10
  10.1 84.7 %copy-start.13 = (s32[8,64,1]{1,2,0:T(1,128)S(1)}, s32[8,64,1]{1,2,0:T(1,128)}, u32[]{:S(2)}) copy-start(s32[8,64,1]{1,2,0:T(1,128)} %param.22) | copy-start | bytes 6148
  10.1 84.8 %copy-start.14 = (s32[8,64]{1,0:T(8,128)S(1)}, s32[8,64]{1,0:T(8,128)}, u32[]{:S(2)}) copy-start(s32[8,64]{1,0:T(8,128)} %param.23) | copy-start | bytes 6148
  88.7 1.2 %copy-start.2 = (f32[3,16,64,128]{3,2,1,0:T(8,128)}, f32[3,16,64,128]{3,2,1,0:T(8,128)S(1)}, u32[]{:S(2)}) copy-start(f32[3,16,64,128]{3,2,1,0:T(8,128)S(1)} %get-tuple-element.12) | copy-start | bytes 4718596
  89.8 10.0 %copy-start.11 = (bf16[32,32,128]{2,1,0:T(8,128)(2,1)S(1)}, bf16[32,32,128]{2,1,0:T(8,128)(2,1)}, u32[]{:S(2)}) copy-start(bf16[32,32,128]{2,1,0:T(8,128)(2,1)} %param.25) | copy-start | bytes 786436
  91.4 8.2 %all-to-all-start = ((f32[8,16,128]{2,1,0:T(8,128)}), f32[8,16,128]{2,1,0:T(8,128)S(1)}, u32[]{:S(2)}, u32[]{:S(2)}) async-start(f32[8,16,128]{2,1,0:T(8,128)} %fusion.8), calls=%async_computation | async-start | bytes 131072 | tf_op jit(solution)/shard_map/all_to_all | solution.py:467
  99.9 3.6 %copy-start.12 = (f32[32,128]{1,0:T(8,128)}, f32[32,128]{1,0:T(8,128)S(1)}, u32[]{:S(2)}) copy-start(f32[32,128]{1,0:T(8,128)S(1)} %convolution_bitcast_fusion.1) | copy-start | bytes 49156
